TPU v7x, 256 devices: a whole 4x4x8 slice. The times are simulated.
256 devices in a mesh: az: 64 (over x, z, core), rg: 4 (over y).
Axes of the slice: x: 4, y: 4, z: 8, core: 2. Of those that a mesh axis runs over, the one named last changes fastest.
Arguments:
- echo_data: float32 [2, 2048, 32768], P(None, 'rg', 'az'), may hold values from -6 to 6
- chirp_phase: float32 [2048], P('rg'), may hold values from -3.140625 to 3.140625
- stolt_shift: int32 [16, 32768], P('rg', 'az'), may hold values from 0 to 64
- tap_index: int32 [16, 32768], P('rg', 'az'), may hold values from 0 to 15
Outputs:
- mapped_spectrum: float32 [2, 2048, 32768], P(None, 'rg', 'az')
All inputs are finite; a program needn't handle non-finite values.
Results may differ from a plain program's by a relative error of at most 0.0003.
Values sent between devices are 32-bit elements; how exact they have to be, the bound alone decides.
A program may use at most 64 MiB of HBM per device.

v0:
```python
import math

import jax
import jax.numpy as jnp
from jax import lax
from jax.sharding import PartitionSpec as P

AZ_DEV = 512
SHIFT_MAX = 64
FRAC_STEPS = 16
TAP_COUNT = 8


def extended_2(shard, sides, width):
    for axis, dim in sides:
        count, length = (lax.axis_size(axis), shard.shape[dim])
        up = [(i, (i + 1) % count) for i in range(count - 1)]
        down = [(j, i) for i, j in up]
        last = lax.slice_in_dim(shard, length - width, length, axis=dim)
        first = lax.slice_in_dim(shard, 0, width, axis=dim)
        before = lax.ppermute(last, axis, up)
        after = lax.ppermute(first, axis, down)
        shard = jnp.concatenate([before, shard, after], axis=dim)
    return shard


def stolt_map(extended, shift_table, tap_table, row_count):
    groups, col_count = shift_table.shape
    seg_len = row_count // groups
    bit_count = max(SHIFT_MAX.bit_length(), 1)
    span = (1 << bit_count) - 1
    window_len = seg_len + TAP_COUNT - 1 + span
    extra = window_len + (groups - 1) * seg_len - extended.shape[1]
    extended = jnp.pad(extended, ((0, 0), (0, extra), (0, 0)))
    windows = jnp.stack(
        [extended[:, group * seg_len : group * seg_len + window_len] for group in range(groups)],
        axis=1,
    )
    for bit in range(bit_count):
        step = 1 << bit
        length = windows.shape[2]
        chosen = (shift_table >> bit & 1 == 1)[None, :, None, :]
        windows = jnp.where(chosen, windows[:, :, step:], windows[:, :, : length - step])
    frac_values = jnp.arange(FRAC_STEPS, dtype=jnp.int32).astype(jnp.float32) * (1.0 / FRAC_STEPS)
    accumulated = jnp.zeros((2, groups, seg_len, col_count), jnp.float32)
    for tap_slot in range(TAP_COUNT):
        offset = tap_slot - 3.0 - frac_values
        table_row = jnp.sinc(offset) * (0.54 + 0.46 * jnp.cos(offset * (math.pi / 4.0)))
        weight = jnp.zeros((groups, col_count), jnp.float32)
        for frac_slot in range(FRAC_STEPS):
            weight = jnp.where(tap_table == frac_slot, table_row[frac_slot], weight)
        picked = windows[:, :, tap_slot : tap_slot + seg_len]
        accumulated = accumulated + weight[None, :, None, :] * picked
    return accumulated.reshape(2, row_count, col_count)


def angle_table(first_count, second_count, modulus):
    first_axis = jnp.arange(first_count, dtype=jnp.int32)[:, None]
    second_axis = jnp.arange(second_count, dtype=jnp.int32)[None, :]
    angles = (first_axis * second_axis % modulus).astype(jnp.float32) * (2.0 * math.pi / modulus)
    return (jnp.cos(angles), jnp.sin(angles))


def contract(form, left, right):
    return jnp.einsum(
        form, left, right, precision=lax.Precision.HIGHEST, preferred_element_type=jnp.float32
    )


def azimuth_dft(signal, tables):
    first_cos, first_sin, twid_cos, twid_sin, second_cos, second_sin = tables
    first_factor = first_cos.shape[0]
    second_factor = second_cos.shape[0]
    count_items = signal.shape[1]
    full_len = first_factor * second_factor
    grid = signal.reshape(2, count_items, first_factor, second_factor)
    real_part = grid[0]
    imag_part = grid[1]
    section_real = contract("nab,ac->ncb", real_part, first_cos) + contract(
        "nab,ac->ncb", imag_part, first_sin
    )
    section_imag = contract("nab,ac->ncb", imag_part, first_cos) - contract(
        "nab,ac->ncb", real_part, first_sin
    )
    turned_real = section_real * twid_cos + section_imag * twid_sin
    turned_imag = section_imag * twid_cos - section_real * twid_sin
    final_real = contract("ncb,bd->ndc", turned_real, second_cos) + contract(
        "ncb,bd->ndc", turned_imag, second_sin
    )
    final_imag = contract("ncb,bd->ndc", turned_imag, second_cos) - contract(
        "ncb,bd->ndc", turned_real, second_sin
    )
    norm_factor = 1.0 / math.sqrt(full_len)
    return jnp.stack([final_real, final_imag]).reshape(2, count_items, full_len) * norm_factor


def on_device(echo_data, chirp_phase, stolt_shift, tap_index):
    rg_rows = echo_data.shape[1]
    az_cols = echo_data.shape[2]
    az_count = lax.axis_size("az")
    full_len = az_cols * az_count
    range_total = rg_rows * lax.axis_size("rg")
    cosine = jnp.cos(chirp_phase)[:, None]
    sine = jnp.sin(chirp_phase)[:, None]
    real_part = echo_data[0] * cosine + echo_data[1] * sine
    imag_part = echo_data[1] * cosine - echo_data[0] * sine
    compressed = jnp.stack([real_part, imag_part])
    bin_groups = rg_rows // az_count
    folded = compressed.reshape(2, bin_groups, az_count, az_cols)
    first_factor = AZ_DEV // 4
    second_factor = full_len // first_factor
    first_cos, first_sin = angle_table(first_factor, first_factor, first_factor)
    twid_cos, twid_sin = angle_table(first_factor, second_factor, full_len)
    second_cos, second_sin = angle_table(second_factor, second_factor, second_factor)
    tables = (first_cos, first_sin, twid_cos, twid_sin, second_cos, second_sin)
    turned = lax.all_to_all(folded, "az", split_axis=2, concat_axis=2, tiled=True)
    count_items = turned.shape[1]
    spectra = azimuth_dft(turned.reshape(2, count_items, full_len), tables)
    returned = lax.all_to_all(
        spectra.reshape(2, count_items, az_count, az_cols),
        "az",
        split_axis=2,
        concat_axis=2,
        tiled=True,
    )
    spectrum = returned.reshape(2, rg_rows, az_cols)
    half_len = full_len // 2
    range_rows = lax.axis_index("rg") * rg_rows + jnp.arange(rg_rows, dtype=jnp.int32)
    range_freq = 1.0 + range_rows.astype(jnp.float32) * (1.0 / range_total)
    lines = lax.axis_index("az") * az_cols + jnp.arange(az_cols, dtype=jnp.int32)
    signed = jnp.where(lines < half_len, lines, lines - full_len)
    azim_freq = signed.astype(jnp.float32) * (0.9 / half_len)
    phase_angle = 40.0 * jnp.sqrt(
        range_freq[:, None] * range_freq[:, None] - azim_freq[None, :] * azim_freq[None, :]
    )
    cos_phase = jnp.cos(phase_angle)
    sin_phase = jnp.sin(phase_angle)
    focus_real = spectrum[0] * cos_phase - spectrum[1] * sin_phase
    focus_imag = spectrum[0] * sin_phase + spectrum[1] * cos_phase
    focused = jnp.stack([focus_real, focus_imag])
    reach = SHIFT_MAX + 4
    padded = extended_2(focused, (("rg", 1),), reach)
    extended = padded[:, reach - 3 :]
    return stolt_map(extended, stolt_shift, tap_index, rg_rows)


def solution(mesh):
    return jax.shard_map(
        on_device,
        mesh=mesh,
        in_specs=(P(None, "rg", "az"), P("rg"), P("rg", "az"), P("rg", "az")),
        out_specs=P(None, "rg", "az"),
        check_vma=False,
    )
```

profile of v0, /device:TPU:1, one launch (start us, length us, event | category | flops | bytes accessed | tf_op | source)
XLA Modules:
  0.0 209.9 jit_solution(18027071107624884537)
XLA Ops:
  0.0 0.7 fusion.148
  0.7 1.8 multiply_add_fusion.1
  2.8 2.5 %copy.22 = f32[2,8,64,512]{3,1,0,2:T(8,128)} copy(f32[2,8,64,512]{3,2,1,0:T(8,128)S(1)} %pad_maximum_fusion.1) | data formatting | bytes 4194304 | tf_op jit(solution)/shard_map/stack | solution.py:107
  5.3 13.2 %all-to-all-start = ((f32[2,8,64,512]{3,1,0,2:T(8,128)}), f32[2,8,64,512]{3,1,0,2:T(8,128)S(1)}, u32[]{:S(2)}, u32[]{:S(2)}) async-start(f32[2,8,64,512]{3,1,0,2:T(8,128)} %copy.22), calls=%async_computation | async-start | bytes 4194304 | tf_op jit(solution)/shard_map/all_to_all | solution.py:116
  19.0 50.5 %all-to-all-done = f32[2,8,64,512]{3,1,0,2:T(8,128)S(1)} async-done(((f32[2,8,64,512]{3,1,0,2:T(8,128)}), f32[2,8,64,512]{3,1,0,2:T(8,128)S(1)}, u32[]{:S(2)}, u32[]{:S(2)}) %all-to-all-start) | async-done | bytes 2097184 | tf_op jit(solution)/shard_map/all_to_all | solution.py:116
  69.6 1.2 fusion.147
  71.5 2.3 %fusion.56 = f32[128,8,256]{2,0,1:T(8,128)} fusion(f32[8,128,256]{2,1,0:T(8,128)S(1)} %squeeze.419), kind=kOutput, calls=%fused_computation.103 | convolution fusion | flops 402882560 | bytes 2097152 | tf_op jit(solution)/shard_map/nab,ac->ncb/dot_general | solution.py:65
  74.6 1.3 fusion.58
  75.9 1.3 convolution_subtract_fusion
  77.2 1.3 convolution_add_fusion
  78.5 2.1 %fusion.25 = f32[256,8,128]{2,0,1:T(8,128)S(1)} fusion(f32[128,8,256]{2,0,1:T(8,128)S(1)} %convolution_subtract_fusion, f32[128,8,256]{2,0,1:T(8,128)S(1)} %convolution_add_fusion, f32[128,256]{1,0:T(8,128)S(1)} %get-tuple-element.174, f32[128,256]{1,0:T(8,128)S(1)} %get-tuple-element.175), kind=kOutput, calls=%fused_computation.60 | convolution fusion | flops 807010304 | bytes 3407872 | tf_op jit(solution)/shard_map/ncb,bd->ndc/dot_general | solution.py:65
  80.6 2.1 %fusion.21 = f32[256,8,128]{2,0,1:T(8,128)S(1)} fusion(f32[128,8,256]{2,0,1:T(8,128)S(1)} %convolution_add_fusion, f32[128,8,256]{2,0,1:T(8,128)S(1)} %convolution_subtract_fusion, f32[128,256]{1,0:T(8,128)S(1)} %get-tuple-element.174, f32[128,256]{1,0:T(8,128)S(1)} %get-tuple-element.175), kind=kOutput, calls=%fused_computation.56 | convolution fusion | flops 807010304 | bytes 3407872 | tf_op jit(solution)/shard_map/ncb,bd->ndc/dot_general | solution.py:65
  82.7 3.3 %fusion.8 = f32[8,256,128]{2,1,0:T(8,128)} fusion(f32[256,8,128]{2,0,1:T(8,128)S(1)} %fusion.25, f32[128,8,256]{2,0,1:T(8,128)S(1)} %convolution_add_fusion, f32[128,8,256]{2,0,1:T(8,128)S(1)} %convolution_subtract_fusion, f32[128,256]{1,0:T(8,128)S(1)} %get-tuple-element.174, f32[128,256]{1,0:T(8,128)S(1)} %get-tuple-element.175), kind=kOutput, calls=%fused_computation.32 | convolution fusion | flops 807272448 | bytes 4456448 | tf_op jit(solution)/shard_map/ncb,bd->ndc/dot_general | solution.py:65
  86.0 2.4 %stack.41 = f32[1,8,64,512]{3,2,1,0:T(8,128)} reshape(f32[8,256,128]{2,1,0:T(8,128)} %fusion.8) | data formatting | bytes 2097152 | tf_op jit(solution)/shard_map/stack | solution.py:94
  88.4 2.8 %copy.25 = f32[1,8,64,512]{3,1,0,2:T(8,128)} copy(f32[1,8,64,512]{3,2,1,0:T(8,128)} %stack.41) | data formatting | bytes 2097152 | tf_op jit(solution)/shard_map/stack | solution.py:94
  91.2 3.1 %fusion.7 = f32[8,256,128]{2,1,0:T(8,128)} fusion(f32[256,8,128]{2,0,1:T(8,128)S(1)} %fusion.21, f32[128,8,256]{2,0,1:T(8,128)S(1)} %convolution_subtract_fusion, f32[128,8,256]{2,0,1:T(8,128)S(1)} %convolution_add_fusion, f32[128,256]{1,0:T(8,128)S(1)} %get-tuple-element.174, f32[128,256]{1,0:T(8,128)S(1)} %get-tuple-element.175), kind=kOutput, calls=%fused_computation.30 | convolution fusion | flops 807272448 | bytes 4456448 | tf_op jit(solution)/shard_map/ncb,bd->ndc/dot_general | solution.py:65
  94.3 1.5 stack.42
  96.4 1.6 maximum_multiply_fusion
  98.0 5.9 %all-to-all-start.1 = ((f32[2,8,64,512]{3,1,0,2:T(8,128)}), f32[2,8,64,512]{3,1,0,2:T(8,128)S(1)}, u32[]{:S(2)}, u32[]{:S(2)}) async-start(f32[2,8,64,512]{3,1,0,2:T(8,128)} %maximum_multiply_fusion), calls=%async_computation.1 | async-start | bytes 4194304 | tf_op jit(solution)/shard_map/all_to_all | solution.py:119
  109.4 10.0 %select_select_fusion.7 = (f32[4,512]{1,0:T(4,128)S(1)}, pred[4,512]{1,0:T(4,128)(4,1)S(1)}, pred[4,512]{1,0:T(4,128)(4,1)S(1)}, pred[4,512]{1,0:T(4,128)(4,1)S(...) fusion(f32[]{:T(128)} %bitcast.15, f32[]{:T(128)} %bitcast.14, ...), kind=kLoop, calls=%fused_computation.128 | loop fusion | flops 65536 | bytes 49216 | tf_op jit(solution)/shard_map/jit(_where)/select_n | solution.py:51
  119.4 9.9 %select_select_fusion = f32[4,512]{1,0:T(4,128)S(1)} fusion(pred[4,512]{1,0:T(4,128)(4,1)S(1)} %get-tuple-element.22, pred[4,512]{1,0:T(4,128)(4,1)S(1)} %get-tuple-element.21, pred[4,512]{1,0:T(4,128)(4,1)S(1)} %get-tuple-element.20, pred[4,512]{1,0:T(4,128)(4,1)S(1)} %get-tuple-element.19, pred[4,512]{1,0:T(4,128)(4,1)S(1)} %get-tuple-element.18, ...), kind=kLoop, calls=%fused_computation.114 | loop fusion | flops 32768 | bytes 41024 | tf_op jit(solution)/shard_map/jit(_where)/select_n | solution.py:51
  129.3 10.0 %select_select_fusion.1 = f32[4,512]{1,0:T(4,128)S(1)} fusion(pred[4,512]{1,0:T(4,128)(4,1)S(1)} %get-tuple-element.22, pred[4,512]{1,0:T(4,128)(4,1)S(1)} %get-tuple-element.21, pred[4,512]{1,0:T(4,128)(4,1)S(1)} %get-tuple-element.20, pred[4,512]{1,0:T(4,128)(4,1)S(1)} %get-tuple-element.19, pred[4,512]{1,0:T(4,128)(4,1)S(1)} %get-tuple-element.18, ...), kind=kLoop, calls=%fused_computation.115 | loop fusion | flops 32768 | bytes 41024 | tf_op jit(solution)/shard_map/jit(_where)/select_n | solution.py:51
  139.3 10.0 %select_select_fusion.2 = f32[4,512]{1,0:T(4,128)S(1)} fusion(pred[4,512]{1,0:T(4,128)(4,1)S(1)} %get-tuple-element.22, pred[4,512]{1,0:T(4,128)(4,1)S(1)} %get-tuple-element.21, pred[4,512]{1,0:T(4,128)(4,1)S(1)} %get-tuple-element.20, pred[4,512]{1,0:T(4,128)(4,1)S(1)} %get-tuple-element.19, pred[4,512]{1,0:T(4,128)(4,1)S(1)} %get-tuple-element.18, ...), kind=kLoop, calls=%fused_computation.116 | loop fusion | flops 32768 | bytes 41024 | tf_op jit(solution)/shard_map/jit(_where)/select_n | solution.py:51
  149.4 9.9 %select_select_fusion.3 = f32[4,512]{1,0:T(4,128)S(1)} fusion(pred[4,512]{1,0:T(4,128)(4,1)S(1)} %get-tuple-element.22, pred[4,512]{1,0:T(4,128)(4,1)S(1)} %get-tuple-element.21, pred[4,512]{1,0:T(4,128)(4,1)S(1)} %get-tuple-element.20, pred[4,512]{1,0:T(4,128)(4,1)S(1)} %get-tuple-element.19, pred[4,512]{1,0:T(4,128)(4,1)S(1)} %get-tuple-element.18, ...), kind=kLoop, calls=%fused_computation.117 | loop fusion | flops 32768 | bytes 41024 | tf_op jit(solution)/shard_map/jit(_where)/select_n | solution.py:51
  159.3 10.0 %select_select_fusion.4 = f32[4,512]{1,0:T(4,128)S(1)} fusion(pred[4,512]{1,0:T(4,128)(4,1)S(1)} %get-tuple-element.22, pred[4,512]{1,0:T(4,128)(4,1)S(1)} %get-tuple-element.21, pred[4,512]{1,0:T(4,128)(4,1)S(1)} %get-tuple-element.20, pred[4,512]{1,0:T(4,128)(4,1)S(1)} %get-tuple-element.19, pred[4,512]{1,0:T(4,128)(4,1)S(1)} %get-tuple-element.18, ...), kind=kLoop, calls=%fused_computation.118 | loop fusion | flops 32768 | bytes 41024 | tf_op jit(solution)/shard_map/jit(_where)/select_n | solution.py:51
  169.4 10.0 %select_select_fusion.5 = f32[4,512]{1,0:T(4,128)S(1)} fusion(pred[4,512]{1,0:T(4,128)(4,1)S(1)} %get-tuple-element.22, pred[4,512]{1,0:T(4,128)(4,1)S(1)} %get-tuple-element.21, pred[4,512]{1,0:T(4,128)(4,1)S(1)} %get-tuple-element.20, pred[4,512]{1,0:T(4,128)(4,1)S(1)} %get-tuple-element.19, pred[4,512]{1,0:T(4,128)(4,1)S(1)} %get-tuple-element.18, ...), kind=kLoop, calls=%fused_computation.119 | loop fusion | flops 32768 | bytes 41024 | tf_op jit(solution)/shard_map/jit(_where)/select_n | solution.py:51
  180.8 4.7 %fusion.19 = (f32[1,512,512]{2,1,0:T(8,128)S(1)}, f32[1,512,512]{2,1,0:T(8,128)S(1)}) fusion(f32[1,8,64,512]{3,2,1,0:T(8,128)S(1)} %copy.31, f32[1,8,64,512]{3,2,1,0:T(8,128)S(1)} %copy.30, f32[512]{0:T(512)S(1)} %get-tuple-element.176, f32[512]{0:T(512)S(1)} %get-tuple-element.177), kind=kLoop, calls=%fused_computation.52 | loop fusion | flops 2097152 | bytes 4198400 | tf_op jit(solution)/shard_map/sub | solution.py:138
  185.5 3.2 %collective-permute-start = (f32[2,68,512]{2,1,0:T(8,128)S(1)}, f32[2,68,512]{2,1,0:T(8,128)S(1)}, u32[]{:S(2)}, u32[]{:S(2)}) collective-permute-start(f32[2,68,512]{2,1,0:T(8,128)S(1)} %get-tuple-element.31), channel_id=1, source_target_pairs={{0,1},{1,2},{2,3},{4,5},{5,6},{6,7},{8,9},{9,10},{10,11},{12,13},{... | collective-permute-start | bytes 835592 | tf_op jit(solution)/shard_map/ppermute | solution.py:21
  188.7 1.6 collective-permute-start.1
  191.0 10.0 %select_select_fusion.6 = f32[4,512]{1,0:T(4,128)S(1)} fusion(pred[4,512]{1,0:T(4,128)(4,1)S(1)} %get-tuple-element.22, pred[4,512]{1,0:T(4,128)(4,1)S(1)} %get-tuple-element.21, pred[4,512]{1,0:T(4,128)(4,1)S(1)} %get-tuple-element.20, pred[4,512]{1,0:T(4,128)(4,1)S(1)} %get-tuple-element.19, pred[4,512]{1,0:T(4,128)(4,1)S(1)} %get-tuple-element.18, ...), kind=kLoop, calls=%fused_computation.120 | loop fusion | flops 32768 | bytes 41024 | tf_op jit(solution)/shard_map/jit(_where)/select_n | solution.py:51
  206.4 2.0 fusion
  208.4 1.6 copy.29
  (51 shorter events, 15.7 us)
Async XLA Ops:
  5.3 64.2 %all-to-all-start = ((f32[2,8,64,512]{3,1,0,2:T(8,128)}), f32[2,8,64,512]{3,1,0,2:T(8,128)S(1)}, u32[]{:S(2)}, u32[]{:S(2)}) async-start(f32[2,8,64,512]{3,1,0,2:T(8,128)} %copy.22), calls=%async_computation | async-start | bytes 4194304 | tf_op jit(solution)/shard_map/all_to_all | solution.py:116
  71.4 2.5 %copy-start.2 = (f32[1,8,64,512]{3,1,0,2:T(8,128)S(1)}, f32[1,8,64,512]{3,1,0,2:T(8,128)}, u32[]{:S(2)}) copy-start(f32[1,8,64,512]{3,1,0,2:T(8,128)} %get-tuple-element.36) | copy-start | bytes 3145732
  74.6 1.3 copy-start
  94.3 2.1 %copy-start.1 = (f32[1,8,64,512]{3,1,0,2:T(8,128)S(1)}, f32[1,8,64,512]{3,1,0,2:T(8,128)}, u32[]{:S(2)}) copy-start(f32[1,8,64,512]{3,1,0,2:T(8,128)} %copy.25) | copy-start | bytes 3145732
  98.0 11.3 %copy-start.4 = (s32[4,512]{1,0:T(4,128)S(1)}, s32[4,512]{1,0:T(4,128)}, u32[]{:S(2)}) copy-start(s32[4,512]{1,0:T(4,128)} %param.7) | copy-start | bytes 24580
  98.0 11.4 %copy-start.3 = (s32[4,512]{1,0:T(4,128)S(1)}, s32[4,512]{1,0:T(4,128)}, u32[]{:S(2)}) copy-start(s32[4,512]{1,0:T(4,128)} %param.8) | copy-start | bytes 24580
  98.0 81.3 %all-to-all-start.1 = ((f32[2,8,64,512]{3,1,0,2:T(8,128)}), f32[2,8,64,512]{3,1,0,2:T(8,128)S(1)}, u32[]{:S(2)}, u32[]{:S(2)}) async-start(f32[2,8,64,512]{3,1,0,2:T(8,128)} %maximum_multiply_fusion), calls=%async_computation.1 | async-start | bytes 4194304 | tf_op jit(solution)/shard_map/all_to_all | solution.py:119
  185.5 15.5 %collective-permute-start = (f32[2,68,512]{2,1,0:T(8,128)S(1)}, f32[2,68,512]{2,1,0:T(8,128)S(1)}, u32[]{:S(2)}, u32[]{:S(2)}) collective-permute-start(f32[2,68,512]{2,1,0:T(8,128)S(1)} %get-tuple-element.31), channel_id=1, source_target_pairs={{0,1},{1,2},{2,3},{4,5},{5,6},{6,7},{8,9},{9,10},{10,11},{12,13},{... | collective-permute-start | bytes 835592 | tf_op jit(solution)/shard_map/ppermute | solution.py:21
  188.7 12.3 %collective-permute-start.1 = (f32[2,68,512]{2,1,0:T(8,128)S(1)}, f32[2,68,512]{2,1,0:T(8,128)S(1)}, u32[]{:S(2)}, u32[]{:S(2)}) collective-permute-start(f32[2,68,512]{2,1,0:T(8,128)S(1)} %get-tuple-element.32), channel_id=1, source_target_pairs={{1,0},{2,1},{3,2},{5,4},{6,5},{7,6},{9,8},{10,9},{11,10},{13,12},{... | collective-permute-start | bytes 835592 | tf_op jit(solution)/shard_map/ppermute | solution.py:22
where the time goes:
time: 212 us; the launch traced here: 210 us
  other arithmetic  96.5 us (46%)
  waiting for transfers between devices  50.5 us (24%)
  starting transfers between devices  23.9 us (11%)
  local copies, waits for them, and re-layouts  21.9 us (10%)
  matrix products  16.8 us (8%)
    select_n x8, other arithmetic, stolt_map(): weight = jnp.where(tap_table == frac_slot, table_row[frac_slot], weight)  79.8 us
    all_to_all x1, waiting for transfers between devices, on_device(): lax.all_to_all(folded, 'az', split_axis=2, concat_axis=2, tiled=True)  50.5 us
    dot_general x8, matrix products, contract(): jnp.einsum(form, left, right, precision=lax.Precision.HIGHEST, preferred_...  16.8 us
    all_to_all x1, starting transfers between devices, on_device(): lax.all_to_all(folded, 'az', split_axis=2, concat_axis=2, tiled=True)  13.2 us
    another operation x4, local copies, waits for them, and re-layouts, azimuth_dft(): jnp.stack([final_real, final_imag]).reshape(2, count_items, full_len)  7.27 us
    all_to_all x1, starting transfers between devices, on_device(): lax.all_to_all(spectra.reshape(2, count_items, az_count, az_cols), 'az',...  5.95 us
    slice x8, local copies, waits for them, and re-layouts, stolt_map(): weight = jnp.where(tap_table == frac_slot, table_row[frac_slot], weight)  5.64 us
    sub x1, other arithmetic, on_device(): focus_real = spectrum[0] * cos_phase - spectrum[1] * sin_phase  4.67 us
  transfers between devices with their start and end apart: 4, of which 1 were waited for; matrix products, arithmetic and copies ran while one was open for 41% of the time, Pallas kernels for 0%

commit v1 on v0

v1 whole, which is shorter than its diff:
```python
import math

import jax
import jax.numpy as jnp
import numpy as np
from jax import lax
from jax.experimental import pallas as pl
from jax.experimental.pallas import tpu as pltpu
from jax.sharding import PartitionSpec as P

MESH = pl.DeviceIdType.MESH
N_AZ = 64
N_RG = 4
ROWS = 512
COLS = 512
FULL = N_AZ * COLS
LANES = 128
FIRST = 256
SECOND = 128
CHUNKS = 4
CHUNK_ROWS = ROWS // CHUNKS
PAIR = CHUNK_ROWS // N_AZ
BLOCK = PAIR * 8
CHUNK_FLAT = N_AZ * BLOCK
FLAT = CHUNKS * CHUNK_FLAT
BEFORE = 8
AFTER = 72
FOCUS_ROWS = BEFORE + ROWS + AFTER + 8
TAPS = 15
EARLY = 7


def split(array):
    high = array.astype(jnp.bfloat16)
    low = (array - np.asarray(high).astype(np.float64)).astype(jnp.bfloat16)
    return high, low


def dft_tables():
    a = np.arange(FIRST)
    angle = 2.0 * np.pi * (np.outer(a, a) % FIRST) / FIRST
    cosine = np.cos(angle).reshape(FIRST, N_AZ, 4)
    sine = np.sin(angle).reshape(FIRST, N_AZ, 4)
    first = np.stack(
        [np.stack([cosine, sine], axis=2), np.stack([-sine, cosine], axis=2)], axis=0
    ).reshape(2 * FIRST, N_AZ * 8)
    angle = 2.0 * np.pi * (np.outer(a, np.arange(SECOND)) % FULL) / FULL
    norm = 1.0 / math.sqrt(FULL)
    twiddle = np.stack([np.cos(angle), np.sin(angle)]) * norm
    b = np.arange(SECOND)
    angle = 2.0 * np.pi * (np.outer(b, b) % SECOND) / SECOND
    cosine = np.cos(angle).reshape(N_AZ, 2, SECOND).transpose(1, 0, 2)
    sine = np.sin(angle).reshape(N_AZ, 2, SECOND).transpose(1, 0, 2)
    second = np.stack(
        [np.concatenate([cosine, sine], axis=2), np.concatenate([-sine, cosine], axis=2)], axis=0
    ).reshape(2 * SECOND, 2 * SECOND)
    first_high, first_low = split(first)
    second_high, second_low = split(second)
    return first_high, first_low, second_high, second_low, twiddle.astype(np.float32)


def sin_cos_of(rest, count):
    sign = 1.0 - 2.0 * (count - 2.0 * jnp.floor(count * 0.5))
    square = rest * rest
    sine = -1.0 / math.factorial(11)
    for order in (9, 7, 5, 3, 1):
        sine = sine * square + (-1.0) ** (order // 2) / math.factorial(order)
    cosine = 1.0 / math.factorial(12)
    for order in (10, 8, 6, 4, 2, 0):
        cosine = cosine * square + (-1.0) ** (order // 2) / math.factorial(order)
    return sine * rest * sign, cosine * sign


def sin_cos(angle):
    count = jnp.floor(angle * (1.0 / math.pi) + 0.5)
    rest = (angle - count * 3.140625) - count * (math.pi - 3.140625)
    return sin_cos_of(rest, count)


def sin_cos_pi(turns):
    count = jnp.floor(turns + 0.5)
    return sin_cos_of((turns - count) * math.pi, count)


def dot3(table_high, table_low, value, contract_on):
    high = value.astype(jnp.bfloat16)
    low = (value - high.astype(jnp.float32)).astype(jnp.bfloat16)
    dims = (((1,), (contract_on,)), ((), ()))
    dot = lambda left, right: lax.dot_general(left, right, dims, preferred_element_type=jnp.float32)
    return dot(table_high, high) + (dot(table_high, low) + dot(table_low, high))


def kernel(
    echo_hbm, chirp_ref, shift_ref, tap_ref, t1h_hbm, t1l_hbm, t2h_hbm, t2l_hbm, tw_hbm,
    out_ref,
    echo, t1h, t1l, t2h, t2l, tw, out_flat, in_flat, spec_flat, back_flat, phase_cos, phase_sin,
    focus, weights, coarse, chirp_cos, chirp_sin, window,
    load_sem, table_sem, send1, recv1, send2, recv2, halo_send, halo_recv,
):
    me = lax.axis_index("az")
    rg = lax.axis_index("rg")
    up = lax.rem(rg + 1, N_RG)
    down = lax.rem(rg + N_RG - 1, N_RG)

    barrier = pltpu.get_barrier_semaphore()

    def greet(i, carry):
        pl.semaphore_signal(
            barrier, inc=1, device_id=(lax.rem(me + i, N_AZ), rg), device_id_type=MESH
        )
        return carry

    echo_copies = []
    for chunk in range(CHUNKS):
        rows = pl.ds(chunk * CHUNK_ROWS, CHUNK_ROWS)
        echo_copies.append(
            pltpu.make_async_copy(echo_hbm.at[:, rows], echo.at[:, rows], load_sem.at[chunk])
        )
        echo_copies[-1].start()
    lax.fori_loop(1, N_AZ, greet, 0)
    for other in (up, down):
        pl.semaphore_signal(barrier, inc=1, device_id=(me, other), device_id_type=MESH)
    table_copies = []
    for index, (source, target) in enumerate(
        ((t1h_hbm, t1h), (t1l_hbm, t1l), (t2h_hbm, t2h), (t2l_hbm, t2l), (tw_hbm, tw))
    ):
        table_copies.append(pltpu.make_async_copy(source, target, table_sem.at[index]))
        table_copies[-1].start()

    sine, cosine = sin_cos_pi(chirp_ref[...] * (1.0 / math.pi))
    for part in range(ROWS // LANES):
        rows = pl.ds(part * LANES, LANES)
        chirp_cos[rows, :] = jnp.transpose(
            jnp.broadcast_to(cosine[part : part + 1, :], (LANES, LANES))
        )
        chirp_sin[rows, :] = jnp.transpose(
            jnp.broadcast_to(sine[part : part + 1, :], (LANES, LANES))
        )

    def matched(chunk):
        def body(i, carry):
            row = pl.multiple_of(chunk * CHUNK_ROWS + i * 8, 8)
            c = chirp_cos[pl.ds(row, 8), :]
            s = chirp_sin[pl.ds(row, 8), :]
            for tile in range(4):
                lanes = slice(tile * LANES, (tile + 1) * LANES)
                re = echo[0, pl.ds(row, 8), lanes]
                im = echo[1, pl.ds(row, 8), lanes]
                out_flat[pl.ds(row * 8 + tile, 8, stride=8), :] = re * c + im * s
                out_flat[pl.ds(row * 8 + 4 + tile, 8, stride=8), :] = im * c - re * s
            return carry

        lax.fori_loop(0, CHUNK_ROWS // 8, body, 0)

    def exchange(source, target, send, recv, chunk):
        def body(i, carry):
            other = lax.rem(me + i, N_AZ)
            away = pl.multiple_of(chunk * CHUNK_FLAT + other * BLOCK, BLOCK)
            home = pl.multiple_of(chunk * CHUNK_FLAT + me * BLOCK, BLOCK)
            pltpu.make_async_remote_copy(
                src_ref=source.at[pl.ds(away, BLOCK)],
                dst_ref=target.at[pl.ds(home, BLOCK)],
                send_sem=send.at[chunk],
                recv_sem=recv.at[chunk],
                device_id=(other, rg),
                device_id_type=MESH,
            ).start()
            return carry

        lax.fori_loop(1, N_AZ, body, 0)
        home = pl.multiple_of(chunk * CHUNK_FLAT + me * BLOCK, BLOCK)
        target[pl.ds(home, BLOCK), :] = source[pl.ds(home, BLOCK), :]

    def all_of(source, target, send, recv, chunk):
        rows = pl.ds(pl.multiple_of(chunk * CHUNK_FLAT, BLOCK), CHUNK_FLAT - BLOCK)
        return pltpu.make_async_remote_copy(
            src_ref=source.at[rows],
            dst_ref=target.at[rows],
            send_sem=send.at[chunk],
            recv_sem=recv.at[chunk],
            device_id=(lax.rem(me + 1, N_AZ), rg),
            device_id_type=MESH,
        )

    for chunk in range(CHUNKS):
        echo_copies[chunk].wait()
        matched(chunk)
        if chunk == 0:
            pl.semaphore_wait(barrier, N_AZ + 1)
        exchange(out_flat, in_flat, send1, recv1, chunk)

    lane_id = lax.broadcasted_iota(jnp.int32, (8, LANES), 1)
    row_id = lax.broadcasted_iota(jnp.int32, (8, LANES), 0)

    def phase_body(i, carry):
        row = pl.multiple_of(i * 8, 8)
        r = 1.0 + (rg * ROWS + row + row_id).astype(jnp.float32) * (1.0 / (ROWS * N_RG))
        rr = r * r
        for tile in range(4):
            line = me * COLS + tile * LANES + lane_id
            signed = jnp.where(line < FULL // 2, line, line - FULL)
            q = signed.astype(jnp.float32) * (0.9 / (FULL // 2))
            s, c = sin_cos(40.0 * jnp.sqrt(rr - q * q))
            phase_cos[tile, pl.ds(row, 8), :] = c
            phase_sin[tile, pl.ds(row, 8), :] = s
        return carry

    lax.fori_loop(0, ROWS // 8, phase_body, 0)

    tap_id = lax.broadcasted_iota(jnp.int32, (16, LANES), 0)
    for seg in range(CHUNKS):
        for tile in range(4):
            lanes = slice(tile * LANES, (tile + 1) * LANES)
            shift = shift_ref[seg : seg + 1, lanes]
            slot = tap_id - jnp.broadcast_to(shift & 7, (16, LANES))
            frac = jnp.broadcast_to(tap_ref[seg : seg + 1, lanes], (16, LANES))
            u = (slot - 3).astype(jnp.float32) - frac.astype(jnp.float32) * (1.0 / 16.0)
            sine, _ = sin_cos_pi(u)
            _, cosine = sin_cos_pi(u * 0.25)
            at_zero = u == 0.0
            sinc = jnp.where(at_zero, 1.0, sine / jnp.where(at_zero, 1.0, u * math.pi))
            inside = jnp.logical_and(slot >= 0, slot < 8)
            weights[seg * 4 + tile] = jnp.where(inside, sinc * (0.54 + 0.46 * cosine), 0.0)
            coarse[seg * 4 + tile] = jnp.broadcast_to(shift >> 3, (8, LANES))

    for plane in range(8):
        focus[plane, pl.ds(BEFORE, ROWS), :] = jnp.zeros((ROWS, LANES), jnp.float32)
        focus[plane, pl.ds(BEFORE + ROWS + AFTER, 8), :] = jnp.zeros((8, LANES), jnp.float32)

    for copy in table_copies:
        copy.wait()

    def transform(chunk, carry):
        all_of(out_flat, in_flat, send1, recv1, chunk).wait_recv()
        start = pl.multiple_of(chunk * CHUNK_FLAT, CHUNK_FLAT)
        both = in_flat[pl.ds(start, CHUNK_FLAT), :].reshape(N_AZ, PAIR, 8, LANES)
        signal = jnp.concatenate(
            [both[:, pair].reshape(N_AZ * 8, LANES) for pair in range(PAIR)], axis=1
        )
        section = dot3(t1h[...], t1l[...], signal, 0)
        for pair in range(PAIR):
            lanes = slice(pair * LANES, (pair + 1) * LANES)
            re = section[:FIRST, lanes]
            im = section[FIRST:, lanes]
            turned = jnp.concatenate([re * tw[0] + im * tw[1], im * tw[0] - re * tw[1]], axis=1)
            final = dot3(t2h[...], t2l[...], turned, 1)
            for quarter in range(4):
                for half in range(2):
                    spec_flat[pl.ds(start + pair * 8 + quarter * 2 + half, N_AZ, stride=BLOCK), :] = (
                        final[quarter * N_AZ : (quarter + 1) * N_AZ, half * LANES : (half + 1) * LANES]
                    )
        exchange(spec_flat, back_flat, send2, recv2, chunk)
        return carry

    lax.fori_loop(0, CHUNKS, transform, 0)

    def focus_rows(chunk):
        all_of(spec_flat, back_flat, send2, recv2, chunk).wait_recv()

        def body(i, carry):
            row = pl.multiple_of(chunk * CHUNK_ROWS + i * 8, 8)
            for tile in range(4):
                a = back_flat[pl.ds(row * 8 + tile, 8, stride=8), :]
                b = back_flat[pl.ds(row * 8 + 4 + tile, 8, stride=8), :]
                c = phase_cos[tile, pl.ds(row, 8), :]
                s = phase_sin[tile, pl.ds(row, 8), :]
                focus[tile, pl.ds(BEFORE + row, 8), :] = a * c - b * s
                focus[4 + tile, pl.ds(BEFORE + row, 8), :] = a * s + b * c
            return carry

        lax.fori_loop(0, CHUNK_ROWS // 8, body, 0)

    def stolt(seg, first, count):
        def body(tile, carry):
            index = seg * 4 + tile
            h = coarse[index]
            eight = h >= 8
            four = (h & 4) != 0
            two = (h & 2) != 0
            one = (h & 1) != 0
            taps = [jnp.broadcast_to(weights[index, m : m + 1, :], (8, LANES)) for m in range(TAPS)]
            for part in range(2):
                plane = part * 4 + tile
                need = count + 3
                base = pl.multiple_of((seg * 16 + first) * 8, 8)
                load = lambda i: focus[plane, pl.ds(base + i * 8, 8), :]
                tiles = [load(i) for i in range(need + 8)]
                step = [
                    jnp.where(eight, tiles[i + 8], tiles[i]) if i < need else tiles[i]
                    for i in range(need + 7)
                ]
                step = [jnp.where(four, step[i + 4], step[i]) for i in range(need + 3)]
                step = [jnp.where(two, step[i + 2], step[i]) for i in range(need + 1)]
                for i in range(need):
                    window[part, i * 8 : i * 8 + 8, :] = jnp.where(one, step[i + 1], step[i])
                for i in range(count):
                    total = None
                    for m in range(TAPS):
                        term = taps[m] * window[part, i * 8 + 5 + m : i * 8 + 13 + m, :]
                        total = term if total is None else total + term
                    out_ref[part, pl.ds(base + i * 8, 8), pl.ds(pl.multiple_of(tile * LANES, LANES), LANES)] = total
            return carry

        lax.fori_loop(0, 4, body, 0)

    def halo(towards, source_row, target_row, count, which):
        return pltpu.make_async_remote_copy(
            src_ref=focus.at[:, pl.ds(source_row, count)],
            dst_ref=focus.at[:, pl.ds(target_row, count)],
            send_sem=halo_send.at[which],
            recv_sem=halo_recv.at[which],
            device_id=(me, towards),
            device_id_type=MESH,
        )

    to_down = halo(down, BEFORE, BEFORE + ROWS, AFTER, 0)
    to_up = halo(up, BEFORE + ROWS - 8, 0, 8, 1)

    focus_rows(0)
    to_down.start()
    stolt(0, 1, EARLY - 1)

    def middle(chunk, carry):
        focus_rows(chunk)
        stolt(chunk - 1, EARLY, 16 - EARLY)
        stolt(chunk, 0, EARLY)
        return carry

    lax.fori_loop(1, CHUNKS - 1, middle, 0)
    focus_rows(CHUNKS - 1)
    to_up.start()
    stolt(CHUNKS - 2, EARLY, 16 - EARLY)
    to_down.wait_recv()

    @pl.when(rg == N_RG - 1)
    def _():
        focus[:, pl.ds(BEFORE + ROWS, AFTER), :] = jnp.zeros((8, AFTER, LANES), jnp.float32)

    stolt(CHUNKS - 1, 0, EARLY)
    stolt(CHUNKS - 1, EARLY, 16 - EARLY)
    to_up.wait_recv()

    @pl.when(rg == 0)
    def _():
        focus[:, pl.ds(0, BEFORE), :] = jnp.zeros((8, BEFORE, LANES), jnp.float32)

    stolt(0, 0, 1)
    to_down.wait_send()
    to_up.wait_send()
    for chunk in range(CHUNKS):
        all_of(out_flat, in_flat, send1, recv1, chunk).wait_send()
        all_of(spec_flat, back_flat, send2, recv2, chunk).wait_send()


def on_device(echo_data, chirp_phase, stolt_shift, tap_index):
    tables = [jnp.asarray(table) for table in dft_tables()]
    any_spec = pl.BlockSpec(memory_space=pl.ANY)
    vmem_spec = pl.BlockSpec(memory_space=pltpu.VMEM)
    f32 = jnp.float32
    return pl.pallas_call(
        kernel,
        out_shape=jax.ShapeDtypeStruct((2, ROWS, COLS), f32),
        in_specs=[any_spec, vmem_spec, vmem_spec, vmem_spec] + [any_spec] * 5,
        out_specs=vmem_spec,
        scratch_shapes=[
            pltpu.VMEM((2, ROWS, COLS), f32),
            pltpu.VMEM((512, 512), jnp.bfloat16),
            pltpu.VMEM((512, 512), jnp.bfloat16),
            pltpu.VMEM((256, 256), jnp.bfloat16),
            pltpu.VMEM((256, 256), jnp.bfloat16),
            pltpu.VMEM((2, FIRST, SECOND), f32),
            pltpu.VMEM((FLAT, LANES), f32),
            pltpu.VMEM((FLAT, LANES), f32),
            pltpu.VMEM((FLAT, LANES), f32),
            pltpu.VMEM((FLAT, LANES), f32),
            pltpu.VMEM((4, ROWS, LANES), f32),
            pltpu.VMEM((4, ROWS, LANES), f32),
            pltpu.VMEM((8, FOCUS_ROWS, LANES), f32),
            pltpu.VMEM((16, 16, LANES), f32),
            pltpu.VMEM((16, 8, LANES), jnp.int32),
            pltpu.VMEM((ROWS, LANES), f32),
            pltpu.VMEM((ROWS, LANES), f32),
            pltpu.VMEM((2, 160, LANES), f32),
            pltpu.SemaphoreType.DMA((CHUNKS,)),
            pltpu.SemaphoreType.DMA((5,)),
            pltpu.SemaphoreType.DMA((CHUNKS,)),
            pltpu.SemaphoreType.DMA((CHUNKS,)),
            pltpu.SemaphoreType.DMA((CHUNKS,)),
            pltpu.SemaphoreType.DMA((CHUNKS,)),
            pltpu.SemaphoreType.DMA((2,)),
            pltpu.SemaphoreType.DMA((2,)),
        ],
        compiler_params=pltpu.CompilerParams(
            collective_id=0, has_side_effects=True, vmem_limit_bytes=48 << 20
        ),
    )(echo_data, chirp_phase.reshape(ROWS // LANES, LANES), stolt_shift, tap_index, *tables)


def solution(mesh):
    return jax.shard_map(
        on_device,
        mesh=mesh,
        in_specs=(P(None, "rg", "az"), P("rg"), P("rg", "az"), P("rg", "az")),
        out_specs=P(None, "rg", "az"),
        check_vma=False,
    )
```

time: 212 us -> 118 us (0.56)
  Pallas kernels: 0 us -> 108 us
  other arithmetic: 96.5 us -> 0 us
  waiting for transfers between devices: 50.5 us -> 0 us
  starting transfers between devices: 23.9 us -> 0 us
  matrix products: 16.8 us -> 0 us
  local copies, waits for them, and re-layouts: 21.9 us -> 9.82 us
    pallas_call x0 -> x1, Pallas kernels: none -> 108 us  [on_device(): pl.pallas_call(kernel, out_shape=jax.ShapeDtypeStruct((2, ROWS, COLS), f3...]
    select_n x15 -> x0, other arithmetic: 83.8 us -> none  [the longest x8 79.8 us: stolt_map(): weight = jnp.where(tap_table == frac_slot, table_row[frac_slot], weight)]
    all_to_all x2 -> x0, waiting for transfers between devices: 50.5 us -> none  [the longest x1 50.5 us: on_device(): lax.all_to_all(folded, 'az', split_axis=2, concat_axis=2, tiled=True)]
    all_to_all x2 -> x0, starting transfers between devices: 19.1 us -> none  [the longest x1 13.2 us: on_device(): lax.all_to_all(folded, 'az', split_axis=2, concat_axis=2, tiled=True)]
    dot_general x8 -> x0, matrix products: 16.8 us -> none  [contract(): jnp.einsum(form, left, right, precision=lax.Precision.HIGHEST, preferred_...]
    another operation x5 -> x0, local copies, waits for them, and re-layouts: 9.8 us -> none  [the longest x4 7.27 us: azimuth_dft(): jnp.stack([final_real, final_imag]).reshape(2, count_items, full_len)]
    unnamed x12 -> x19, local copies, waits for them, and re-layouts: 1.25 us -> 9.82 us
    slice x12 -> x0, local copies, waits for them, and re-layouts: 8.21 us -> none  [the longest x8 5.64 us: stolt_map(): weight = jnp.where(tap_table == frac_slot, table_row[frac_slot], weight)]
  transfers between devices with their start and end apart: 4 -> 0, of which waited for: 1 -> 0; matrix products, arithmetic and copies ran while one was open for 41% -> 0% of each run, Pallas kernels for 0% -> 0%
where the time goes in v1:
time: 118 us
  Pallas kernels  108 us (92%)
  local copies, waits for them, and re-layouts  9.82 us (8%)
    pallas_call x1, Pallas kernels, on_device(): pl.pallas_call(kernel, out_shape=jax.ShapeDtypeStruct((2, ROWS, COLS), f3...  108 us
    unnamed x19, local copies, waits for them, and re-layouts  9.82 us

profile of v1, /device:TPU:1, one launch (start us, length us, event | category | flops | bytes accessed | tf_op | source)
XLA Modules:
  0.0 117.6 jit_solution(14221676648290570571)
XLA Ops:
  0.0 0.0 copy-start
  0.0 1.6 %copy-done = f32[2,512,512]{2,1,0:T(8,128)S(1)} copy-done((f32[2,512,512]{2,1,0:T(8,128)S(1)}, f32[2,512,512]{2,1,0:T(8,128)}, u32[]{:S(2)}) %copy-start) | copy-done | bytes 2097176
  1.6 0.0 copy-start.1
  1.6 1.0 copy-done.1
  2.6 0.0 copy-start.2
  2.6 1.0 copy-done.2
  3.7 0.0 copy-start.3
  3.7 0.9 copy-done.3
  4.6 0.0 copy-start.4
  4.6 0.9 copy-done.4
  5.5 0.0 copy-start.5
  5.5 0.9 copy-done.5
  6.4 0.0 copy-start.6
  6.4 0.7 copy-done.6
  7.1 0.0 copy-start.7
  7.1 0.7 copy-done.7
  7.8 0.0 copy-start.8
  7.8 0.7 copy-done.8
  8.5 107.8 %shard_map.91 = f32[2,512,512]{2,1,0:T(8,128)S(1)} custom-call(f32[2,512,512]{2,1,0:T(8,128)S(1)} %copy-done, f32[4,128]{1,0:T(4,128)S(1)} %bitcast.1, s32[4,512]{1,0:T(4,128)S(1)} %copy-done.6, s32[4,512]{1,0:T(4,128)S(1)} %copy-done.7, bf16[512,512]{1,0:T(8,128)(2,1)S(1)} %copy-done.2, bf16[512,512]{1,0:T(8,128)(2,1)S(1)} %copy-done.1, ...), custom_call_target="tpu_custom_call" | custom-call | tf_op jit(solution)/shard_map/pallas_call | solution.py:360
  116.3 1.3 %copy.11 = f32[2,512,512]{2,1,0:T(8,128)} copy(f32[2,512,512]{2,1,0:T(8,128)S(1)} %shard_map.91) | data formatting | bytes 4194304
Async XLA Ops:
  0.0 1.6 %copy-start = (f32[2,512,512]{2,1,0:T(8,128)S(1)}, f32[2,512,512]{2,1,0:T(8,128)}, u32[]{:S(2)}) copy-start(f32[2,512,512]{2,1,0:T(8,128)} %echo_hbm.1) | copy-start | bytes 6291460
  1.6 1.0 copy-start.1
  2.6 1.0 copy-start.2
  3.7 0.9 copy-start.3
  4.6 0.9 copy-start.4
  5.5 0.9 copy-start.5
  6.4 0.7 copy-start.6
  7.1 0.7 copy-start.7
  7.8 0.7 copy-start.8

commit v2 on v1

--- a/solution.py
+++ b/solution.py
@@ -91,11 +91,11 @@
 
 
 def kernel(
-    echo_hbm, chirp_ref, shift_ref, tap_ref, t1h_hbm, t1l_hbm, t2h_hbm, t2l_hbm, tw_hbm,
-    out_ref,
-    echo, t1h, t1l, t2h, t2l, tw, out_flat, in_flat, spec_flat, back_flat, phase_cos, phase_sin,
+    echo_hbm, chirp_hbm, shift_hbm, tap_hbm, t1h_hbm, t1l_hbm, t2h_hbm, t2l_hbm, tw_hbm,
+    out_hbm,
+    out_ref, echo, chirp_ref, shift_ref, tap_ref, t1h, t1l, t2h, t2l, tw, out_flat, in_flat, spec_flat, back_flat, phase_cos, phase_sin,
     focus, weights, coarse, chirp_cos, chirp_sin, window,
-    load_sem, table_sem, send1, recv1, send2, recv2, halo_send, halo_recv,
+    load_sem, table_sem, store_sem, send1, recv1, send2, recv2, halo_send, halo_recv,
 ):
     me = lax.axis_index("az")
     rg = lax.axis_index("rg")
@@ -110,6 +110,8 @@
         )
         return carry
 
+    chirp_copy = pltpu.make_async_copy(chirp_hbm, chirp_ref, table_sem.at[5])
+    chirp_copy.start()
     echo_copies = []
     for chunk in range(CHUNKS):
         rows = pl.ds(chunk * CHUNK_ROWS, CHUNK_ROWS)
@@ -122,11 +124,19 @@
         pl.semaphore_signal(barrier, inc=1, device_id=(me, other), device_id_type=MESH)
     table_copies = []
     for index, (source, target) in enumerate(
-        ((t1h_hbm, t1h), (t1l_hbm, t1l), (t2h_hbm, t2h), (t2l_hbm, t2l), (tw_hbm, tw))
+        (
+            (t1h_hbm, t1h), (t1l_hbm, t1l), (t2h_hbm, t2h), (t2l_hbm, t2l), (tw_hbm, tw),
+        )
     ):
         table_copies.append(pltpu.make_async_copy(source, target, table_sem.at[index]))
         table_copies[-1].start()
 
+    shift_copy = pltpu.make_async_copy(shift_hbm, shift_ref, table_sem.at[6])
+    tap_copy = pltpu.make_async_copy(tap_hbm, tap_ref, table_sem.at[7])
+    shift_copy.start()
+    tap_copy.start()
+
+    chirp_copy.wait()
     sine, cosine = sin_cos_pi(chirp_ref[...] * (1.0 / math.pi))
     for part in range(ROWS // LANES):
         rows = pl.ds(part * LANES, LANES)
@@ -207,6 +217,8 @@
 
     lax.fori_loop(0, ROWS // 8, phase_body, 0)
 
+    shift_copy.wait()
+    tap_copy.wait()
     tap_id = lax.broadcasted_iota(jnp.int32, (16, LANES), 0)
     for seg in range(CHUNKS):
         for tile in range(4):
@@ -302,6 +314,14 @@
             return carry
 
         lax.fori_loop(0, 4, body, 0)
+        store(seg, first, count).start()
+
+    def store(seg, first, count):
+        rows = pl.ds(pl.multiple_of((seg * 16 + first) * 8, 8), count * 8)
+        which = 2 * seg + (1 if first == EARLY else 0) if first + count > 1 else 2 * CHUNKS
+        return pltpu.make_async_copy(
+            out_ref.at[:, rows], out_hbm.at[:, rows], store_sem.at[which]
+        )
 
     def halo(towards, source_row, target_row, count, which):
         return pltpu.make_async_remote_copy(
@@ -345,6 +365,12 @@
         focus[:, pl.ds(0, BEFORE), :] = jnp.zeros((8, BEFORE, LANES), jnp.float32)
 
     stolt(0, 0, 1)
+    store(0, 0, 1).wait()
+    store(0, 1, EARLY - 1).wait()
+    store(0, EARLY, 16 - EARLY).wait()
+    for seg in range(1, CHUNKS):
+        store(seg, 0, EARLY).wait()
+        store(seg, EARLY, 16 - EARLY).wait()
     to_down.wait_send()
     to_up.wait_send()
     for chunk in range(CHUNKS):
@@ -354,16 +380,19 @@
 
 def on_device(echo_data, chirp_phase, stolt_shift, tap_index):
     tables = [jnp.asarray(table) for table in dft_tables()]
-    any_spec = pl.BlockSpec(memory_space=pl.ANY)
-    vmem_spec = pl.BlockSpec(memory_space=pltpu.VMEM)
+    hbm_spec = pl.BlockSpec(memory_space=pltpu.HBM)
     f32 = jnp.float32
     return pl.pallas_call(
         kernel,
         out_shape=jax.ShapeDtypeStruct((2, ROWS, COLS), f32),
-        in_specs=[any_spec, vmem_spec, vmem_spec, vmem_spec] + [any_spec] * 5,
-        out_specs=vmem_spec,
+        in_specs=[hbm_spec] * 9,
+        out_specs=hbm_spec,
         scratch_shapes=[
             pltpu.VMEM((2, ROWS, COLS), f32),
+            pltpu.VMEM((2, ROWS, COLS), f32),
+            pltpu.VMEM((ROWS // LANES, LANES), f32),
+            pltpu.VMEM((CHUNKS, COLS), jnp.int32),
+            pltpu.VMEM((CHUNKS, COLS), jnp.int32),
             pltpu.VMEM((512, 512), jnp.bfloat16),
             pltpu.VMEM((512, 512), jnp.bfloat16),
             pltpu.VMEM((256, 256), jnp.bfloat16),
@@ -382,7 +411,8 @@
             pltpu.VMEM((ROWS, LANES), f32),
             pltpu.VMEM((2, 160, LANES), f32),
             pltpu.SemaphoreType.DMA((CHUNKS,)),
-            pltpu.SemaphoreType.DMA((5,)),
+            pltpu.SemaphoreType.DMA((8,)),
+            pltpu.SemaphoreType.DMA((2 * CHUNKS + 1,)),
             pltpu.SemaphoreType.DMA((CHUNKS,)),
             pltpu.SemaphoreType.DMA((CHUNKS,)),
             pltpu.SemaphoreType.DMA((CHUNKS,)),
@@ -391,7 +421,7 @@
             pltpu.SemaphoreType.DMA((2,)),
         ],
         compiler_params=pltpu.CompilerParams(
-            collective_id=0, has_side_effects=True, vmem_limit_bytes=48 << 20
+            collective_id=0, has_side_effects=True, vmem_limit_bytes=58 << 20
         ),
     )(echo_data, chirp_phase.reshape(ROWS // LANES, LANES), stolt_shift, tap_index, *tables)
 

time: 118 us -> 112 us (0.949)
  local copies, waits for them, and re-layouts: 9.82 us -> 3.08 us
    unnamed x19 -> x1, local copies, waits for them, and re-layouts: 9.82 us -> 3.08 us
where the time goes in v2:
time: 112 us; the launch traced here: 111 us
  Pallas kernels  108 us (96%)
  local copies, waits for them, and re-layouts  3.08 us (3%)
    pallas_call x1, Pallas kernels, on_device(): pl.pallas_call(kernel, out_shape=jax.ShapeDtypeStruct((2, ROWS, COLS), f3...  108 us
    unnamed x1, local copies, waits for them, and re-layouts  3.08 us

profile of v2, /device:TPU:1, one launch (start us, length us, event | category | flops | bytes accessed | tf_op | source)
XLA Modules:
  0.0 111.4 jit_solution(9296288331466501212)
XLA Ops:
  0.0 108.3 %shard_map.91 = f32[2,512,512]{2,1,0:T(8,128)} custom-call(f32[2,512,512]{2,1,0:T(8,128)} %echo_hbm.1, f32[4,128]{1,0:T(4,128)} %bitcast.1, s32[4,512]{1,0:T(4,128)} %shift_hbm.1, s32[4,512]{1,0:T(4,128)} %tap_hbm.1, bf16[512,512]{1,0:T(8,128)(2,1)} %constant.10.clone.t1h_hbm, bf16[512,512]{1,0:T(8,128)(2,1)} %constant.11.clone.t1l_hbm, ...), custom_call_target="tpu_custom_call" | custom-call | tf_op jit(solution)/shard_map/pallas_call | solution.py:385
  108.3 3.1 %copy.11 = f32[2,512,512]{2,1,0:T(8,128)} copy(f32[2,512,512]{2,1,0:T(8,128)} %shard_map.91) | data formatting | bytes 4194304

commit v3 on v2

--- a/solution.py
+++ b/solution.py
@@ -162,7 +162,7 @@
 
         lax.fori_loop(0, CHUNK_ROWS // 8, body, 0)
 
-    def exchange(source, target, send, recv, chunk):
+    def exchange(source, target, send, recv, chunk, beside=None):
         def body(i, carry):
             other = lax.rem(me + i, N_AZ)
             away = pl.multiple_of(chunk * CHUNK_FLAT + other * BLOCK, BLOCK)
@@ -175,6 +175,8 @@
                 device_id=(other, rg),
                 device_id_type=MESH,
             ).start()
+            if beside is not None:
+                beside(i - 1)
             return carry
 
         lax.fori_loop(1, N_AZ, body, 0)
@@ -192,12 +194,16 @@
             device_id_type=MESH,
         )
 
-    for chunk in range(CHUNKS):
+    echo_copies[0].wait()
+    matched(0)
+    pl.semaphore_wait(barrier, N_AZ + 1)
+    exchange(out_flat, in_flat, send1, recv1, 0)
+    echo_copies[3].wait()
+    matched(3)
+    exchange(out_flat, in_flat, send1, recv1, 3)
+    for chunk in (2, 1):
         echo_copies[chunk].wait()
         matched(chunk)
-        if chunk == 0:
-            pl.semaphore_wait(barrier, N_AZ + 1)
-        exchange(out_flat, in_flat, send1, recv1, chunk)
 
     lane_id = lax.broadcasted_iota(jnp.int32, (8, LANES), 1)
     row_id = lax.broadcasted_iota(jnp.int32, (8, LANES), 0)
@@ -242,7 +248,7 @@
     for copy in table_copies:
         copy.wait()
 
-    def transform(chunk, carry):
+    def transform(chunk):
         all_of(out_flat, in_flat, send1, recv1, chunk).wait_recv()
         start = pl.multiple_of(chunk * CHUNK_FLAT, CHUNK_FLAT)
         both = in_flat[pl.ds(start, CHUNK_FLAT), :].reshape(N_AZ, PAIR, 8, LANES)
@@ -262,9 +268,6 @@
                         final[quarter * N_AZ : (quarter + 1) * N_AZ, half * LANES : (half + 1) * LANES]
                     )
         exchange(spec_flat, back_flat, send2, recv2, chunk)
-        return carry
-
-    lax.fori_loop(0, CHUNKS, transform, 0)
 
     def focus_rows(chunk):
         all_of(spec_flat, back_flat, send2, recv2, chunk).wait_recv()
@@ -318,58 +321,88 @@
 
     def store(seg, first, count):
         rows = pl.ds(pl.multiple_of((seg * 16 + first) * 8, 8), count * 8)
-        which = 2 * seg + (1 if first == EARLY else 0) if first + count > 1 else 2 * CHUNKS
+        which = 2 * seg + (1 if first == EARLY else 0) if count > 1 else 2 * CHUNKS + seg - 2
         return pltpu.make_async_copy(
             out_ref.at[:, rows], out_hbm.at[:, rows], store_sem.at[which]
         )
 
-    def halo(towards, source_row, target_row, count, which):
-        return pltpu.make_async_remote_copy(
-            src_ref=focus.at[:, pl.ds(source_row, count)],
-            dst_ref=focus.at[:, pl.ds(target_row, count)],
-            send_sem=halo_send.at[which],
-            recv_sem=halo_recv.at[which],
-            device_id=(me, towards),
-            device_id_type=MESH,
-        )
-
-    to_down = halo(down, BEFORE, BEFORE + ROWS, AFTER, 0)
-    to_up = halo(up, BEFORE + ROWS - 8, 0, 8, 1)
-
-    focus_rows(0)
-    to_down.start()
-    stolt(0, 1, EARLY - 1)
-
-    def middle(chunk, carry):
-        focus_rows(chunk)
-        stolt(chunk - 1, EARLY, 16 - EARLY)
-        stolt(chunk, 0, EARLY)
+    def halo(towards, source_row, target_row, which):
+        def piece(plane, start, count):
+            return pltpu.make_async_remote_copy(
+                src_ref=focus.at[plane, pl.ds(source_row + start, count)],
+                dst_ref=focus.at[plane, pl.ds(target_row + start, count)],
+                send_sem=halo_send.at[which],
+                recv_sem=halo_recv.at[which],
+                device_id=(me, towards),
+                device_id_type=MESH,
+            )
+
+        return piece
+
+    down_piece = halo(down, BEFORE, BEFORE + ROWS, 0)
+    up_piece = halo(up, BEFORE + ROWS - BEFORE, 0, 1)
+    to_down = down_piece(slice(None), 0, AFTER)
+    to_up = up_piece(slice(None), 0, BEFORE)
+
+    def send_down(piece):
+        down_piece(piece // 9, pl.multiple_of(piece % 9 * 8, 8), 8).start()
+
+    def step(k, carry):
+        now = (CHUNKS - k) % CHUNKS
+        transform(now)
+
+        @pl.when(k == 0)
+        def _():
+            exchange(out_flat, in_flat, send1, recv1, 2)
+
+        @pl.when(k >= 1)
+        def _():
+            focus_rows((CHUNKS + 1 - k) % CHUNKS)
+
+        @pl.when(k == 1)
+        def _():
+            exchange(out_flat, in_flat, send1, recv1, 1, beside=send_down)
+            for piece in range(N_AZ - 1, 72):
+                send_down(piece)
+
+        @pl.when(k == 2)
+        def _():
+            for plane in range(8):
+                up_piece(plane, 0, BEFORE).start()
+            to_down.wait_recv()
+
+            @pl.when(rg == N_RG - 1)
+            def _():
+                focus[:, pl.ds(BEFORE + ROWS, AFTER), :] = jnp.zeros((8, AFTER, LANES), jnp.float32)
+
+        @pl.when(k >= 2)
+        def _():
+            seg = CHUNKS + 1 - k
+            stolt(seg, 1, EARLY - 1)
+            stolt(seg, EARLY, 16 - EARLY)
+
         return carry
 
-    lax.fori_loop(1, CHUNKS - 1, middle, 0)
-    focus_rows(CHUNKS - 1)
-    to_up.start()
-    stolt(CHUNKS - 2, EARLY, 16 - EARLY)
-    to_down.wait_recv()
-
-    @pl.when(rg == N_RG - 1)
-    def _():
-        focus[:, pl.ds(BEFORE + ROWS, AFTER), :] = jnp.zeros((8, AFTER, LANES), jnp.float32)
-
-    stolt(CHUNKS - 1, 0, EARLY)
-    stolt(CHUNKS - 1, EARLY, 16 - EARLY)
+    lax.fori_loop(0, CHUNKS, step, 0)
+    stolt(3, 0, 1)
     to_up.wait_recv()
 
     @pl.when(rg == 0)
     def _():
         focus[:, pl.ds(0, BEFORE), :] = jnp.zeros((8, BEFORE, LANES), jnp.float32)
 
-    stolt(0, 0, 1)
-    store(0, 0, 1).wait()
-    store(0, 1, EARLY - 1).wait()
-    store(0, EARLY, 16 - EARLY).wait()
-    for seg in range(1, CHUNKS):
-        store(seg, 0, EARLY).wait()
+    stolt(0, 0, EARLY)
+    focus_rows(1)
+    stolt(0, EARLY, 16 - EARLY)
+    stolt(1, 0, EARLY)
+    stolt(1, EARLY, 16 - EARLY)
+    stolt(2, 0, 1)
+    for seg in range(CHUNKS):
+        if seg < 2:
+            store(seg, 0, EARLY).wait()
+        else:
+            store(seg, 0, 1).wait()
+            store(seg, 1, EARLY - 1).wait()
         store(seg, EARLY, 16 - EARLY).wait()
     to_down.wait_send()
     to_up.wait_send()
@@ -412,7 +445,7 @@
             pltpu.VMEM((2, 160, LANES), f32),
             pltpu.SemaphoreType.DMA((CHUNKS,)),
             pltpu.SemaphoreType.DMA((8,)),
-            pltpu.SemaphoreType.DMA((2 * CHUNKS + 1,)),
+            pltpu.SemaphoreType.DMA((2 * CHUNKS + 2,)),
             pltpu.SemaphoreType.DMA((CHUNKS,)),
             pltpu.SemaphoreType.DMA((CHUNKS,)),
             pltpu.SemaphoreType.DMA((CHUNKS,)),

time: 112 us -> 109 us (0.973)
  Pallas kernels: 108 us -> 105 us
    pallas_call x1, Pallas kernels: 108 us -> 105 us  [on_device(): pl.pallas_call(kernel, out_shape=jax.ShapeDtypeStruct((2, ROWS, COLS), f3...]
where the time goes in v3:
time: 109 us
  Pallas kernels  105 us (96%)
  local copies, waits for them, and re-layouts  3.08 us (3%)
    pallas_call x1, Pallas kernels, on_device(): pl.pallas_call(kernel, out_shape=jax.ShapeDtypeStruct((2, ROWS, COLS), f3...  105 us
    unnamed x1, local copies, waits for them, and re-layouts  3.08 us

profile of v3, /device:TPU:1, one launch (start us, length us, event | category | flops | bytes accessed | tf_op | source)
XLA Modules:
  0.0 108.5 jit_solution(17488927845939365007)
XLA Ops:
  0.0 105.5 %shard_map.91 = f32[2,512,512]{2,1,0:T(8,128)} custom-call(f32[2,512,512]{2,1,0:T(8,128)} %echo_hbm.1, f32[4,128]{1,0:T(4,128)} %bitcast.1, s32[4,512]{1,0:T(4,128)} %shift_hbm.1, s32[4,512]{1,0:T(4,128)} %tap_hbm.1, bf16[512,512]{1,0:T(8,128)(2,1)} %constant.10.clone.t1h_hbm, bf16[512,512]{1,0:T(8,128)(2,1)} %constant.11.clone.t1l_hbm, ...), custom_call_target="tpu_custom_call" | custom-call | tf_op jit(solution)/shard_map/pallas_call | solution.py:418
  105.5 3.1 %copy.11 = f32[2,512,512]{2,1,0:T(8,128)} copy(f32[2,512,512]{2,1,0:T(8,128)} %shard_map.91) | data formatting | bytes 4194304

commit v4 on v3

--- a/solution.py
+++ b/solution.py
@@ -92,10 +92,10 @@
 
 def kernel(
     echo_hbm, chirp_hbm, shift_hbm, tap_hbm, t1h_hbm, t1l_hbm, t2h_hbm, t2l_hbm, tw_hbm,
-    out_hbm,
-    out_ref, echo, chirp_ref, shift_ref, tap_ref, t1h, t1l, t2h, t2l, tw, out_flat, in_flat, spec_flat, back_flat, phase_cos, phase_sin,
+    out_ref,
+    echo, chirp_ref, shift_ref, tap_ref, t1h, t1l, t2h, t2l, tw, out_flat, in_flat, spec_flat, back_flat, phase_cos, phase_sin,
     focus, weights, coarse, chirp_cos, chirp_sin, window,
-    load_sem, table_sem, store_sem, send1, recv1, send2, recv2, halo_send, halo_recv,
+    load_sem, table_sem, send1, recv1, send2, recv2, halo_send, halo_recv,
 ):
     me = lax.axis_index("az")
     rg = lax.axis_index("rg")
@@ -317,14 +317,6 @@
             return carry
 
         lax.fori_loop(0, 4, body, 0)
-        store(seg, first, count).start()
-
-    def store(seg, first, count):
-        rows = pl.ds(pl.multiple_of((seg * 16 + first) * 8, 8), count * 8)
-        which = 2 * seg + (1 if first == EARLY else 0) if count > 1 else 2 * CHUNKS + seg - 2
-        return pltpu.make_async_copy(
-            out_ref.at[:, rows], out_hbm.at[:, rows], store_sem.at[which]
-        )
 
     def halo(towards, source_row, target_row, which):
         def piece(plane, start, count):
@@ -397,13 +389,6 @@
     stolt(1, 0, EARLY)
     stolt(1, EARLY, 16 - EARLY)
     stolt(2, 0, 1)
-    for seg in range(CHUNKS):
-        if seg < 2:
-            store(seg, 0, EARLY).wait()
-        else:
-            store(seg, 0, 1).wait()
-            store(seg, 1, EARLY - 1).wait()
-        store(seg, EARLY, 16 - EARLY).wait()
     to_down.wait_send()
     to_up.wait_send()
     for chunk in range(CHUNKS):
@@ -415,13 +400,17 @@
     tables = [jnp.asarray(table) for table in dft_tables()]
     hbm_spec = pl.BlockSpec(memory_space=pltpu.HBM)
     f32 = jnp.float32
+    chirp = chirp_phase.reshape(ROWS // LANES, LANES)
+    operands = [
+        pltpu.with_memory_space_constraint(operand, pltpu.HBM)
+        for operand in (echo_data, chirp, stolt_shift, tap_index, *tables)
+    ]
     return pl.pallas_call(
         kernel,
-        out_shape=jax.ShapeDtypeStruct((2, ROWS, COLS), f32),
+        out_shape=pltpu.VMEM((2, ROWS, COLS), f32),
         in_specs=[hbm_spec] * 9,
-        out_specs=hbm_spec,
+        out_specs=pl.BlockSpec(memory_space=pltpu.VMEM),
         scratch_shapes=[
-            pltpu.VMEM((2, ROWS, COLS), f32),
             pltpu.VMEM((2, ROWS, COLS), f32),
             pltpu.VMEM((ROWS // LANES, LANES), f32),
             pltpu.VMEM((CHUNKS, COLS), jnp.int32),
@@ -445,7 +434,6 @@
             pltpu.VMEM((2, 160, LANES), f32),
             pltpu.SemaphoreType.DMA((CHUNKS,)),
             pltpu.SemaphoreType.DMA((8,)),
-            pltpu.SemaphoreType.DMA((2 * CHUNKS + 2,)),
             pltpu.SemaphoreType.DMA((CHUNKS,)),
             pltpu.SemaphoreType.DMA((CHUNKS,)),
             pltpu.SemaphoreType.DMA((CHUNKS,)),
@@ -454,9 +442,9 @@
             pltpu.SemaphoreType.DMA((2,)),
         ],
         compiler_params=pltpu.CompilerParams(
-            collective_id=0, has_side_effects=True, vmem_limit_bytes=58 << 20
+            collective_id=0, has_side_effects=True, vmem_limit_bytes=50 << 20
         ),
-    )(echo_data, chirp_phase.reshape(ROWS // LANES, LANES), stolt_shift, tap_index, *tables)
+    )(*operands)
 
 
 def solution(mesh):

time: 109 us -> 106 us (0.972)
  local copies, waits for them, and re-layouts: 3.08 us -> 1.32 us
    unnamed x1, local copies, waits for them, and re-layouts: 3.08 us -> 1.32 us
where the time goes in v4:
time: 106 us
  Pallas kernels  105 us (99%)
  local copies, waits for them, and re-layouts  1.32 us (1%)
    pallas_call x1, Pallas kernels, on_device(): pl.pallas_call(kernel, out_shape=pltpu.VMEM((2, ROWS, COLS), f32), in_spe...  105 us

profile of v4, /device:TPU:1, one launch (start us, length us, event | category | flops | bytes accessed | tf_op | source)
XLA Modules:
  0.0 106.1 jit_solution(6116321571053178343)
XLA Ops:
  0.0 104.7 %shard_map.91 = f32[2,512,512]{2,1,0:T(8,128)S(1)} custom-call(f32[2,512,512]{2,1,0:T(8,128)} %echo_hbm.1, f32[4,128]{1,0:T(4,128)} %bitcast.1, s32[4,512]{1,0:T(4,128)} %shift_hbm.1, s32[4,512]{1,0:T(4,128)} %tap_hbm.1, bf16[512,512]{1,0:T(8,128)(2,1)} %constant.10.clone.t1h_hbm, bf16[512,512]{1,0:T(8,128)(2,1)} %constant.11.clone.t1l_hbm, ...), custom_call_target="tpu_custom_call" | custom-call | tf_op jit(solution)/shard_map/pallas_call | solution.py:408
  104.8 1.3 %copy.11 = f32[2,512,512]{2,1,0:T(8,128)} copy(f32[2,512,512]{2,1,0:T(8,128)S(1)} %shard_map.91) | data formatting | bytes 4194304

commit v5 on v4

--- a/solution.py
+++ b/solution.py
@@ -90,11 +90,45 @@
     return dot(table_high, high) + (dot(table_high, low) + dot(table_low, high))
 
 
+def map_rows(out_ref, focus, weights, coarse, window, seg, first, count):
+    def body(tile, carry):
+        index = seg * 4 + tile
+        h = coarse[index]
+        eight = h >= 8
+        four = (h & 4) != 0
+        two = (h & 2) != 0
+        one = (h & 1) != 0
+        taps = [jnp.broadcast_to(weights[index, m : m + 1, :], (8, LANES)) for m in range(TAPS)]
+        for part in range(2):
+            plane = part * 4 + tile
+            need = count + 3
+            base = (seg * 16 + first) * 8 if isinstance(seg, int) else pl.multiple_of((seg * 16 + first) * 8, 8)
+            load = lambda i: focus[plane, pl.ds(base + i * 8, 8), :]
+            tiles = [load(i) for i in range(need + 8)]
+            step = [
+                jnp.where(eight, tiles[i + 8], tiles[i]) if i < need else tiles[i]
+                for i in range(need + 7)
+            ]
+            step = [jnp.where(four, step[i + 4], step[i]) for i in range(need + 3)]
+            step = [jnp.where(two, step[i + 2], step[i]) for i in range(need + 1)]
+            for i in range(need):
+                window[part, i * 8 : i * 8 + 8, :] = jnp.where(one, step[i + 1], step[i])
+            for i in range(count):
+                total = None
+                for m in range(TAPS):
+                    term = taps[m] * window[part, i * 8 + 5 + m : i * 8 + 13 + m, :]
+                    total = term if total is None else total + term
+                out_ref[part, pl.ds(base + i * 8, 8), pl.ds(pl.multiple_of(tile * LANES, LANES), LANES)] = total
+        return carry
+
+    lax.fori_loop(0, 4, body, 0)
+
+
 def kernel(
     echo_hbm, chirp_hbm, shift_hbm, tap_hbm, t1h_hbm, t1l_hbm, t2h_hbm, t2l_hbm, tw_hbm,
-    out_ref,
+    out_ref, focus, weights, coarse,
     echo, chirp_ref, shift_ref, tap_ref, t1h, t1l, t2h, t2l, tw, out_flat, in_flat, spec_flat, back_flat, phase_cos, phase_sin,
-    focus, weights, coarse, chirp_cos, chirp_sin, window,
+    chirp_cos, chirp_sin, window,
     load_sem, table_sem, send1, recv1, send2, recv2, halo_send, halo_recv,
 ):
     me = lax.axis_index("az")
@@ -286,37 +320,7 @@
         lax.fori_loop(0, CHUNK_ROWS // 8, body, 0)
 
     def stolt(seg, first, count):
-        def body(tile, carry):
-            index = seg * 4 + tile
-            h = coarse[index]
-            eight = h >= 8
-            four = (h & 4) != 0
-            two = (h & 2) != 0
-            one = (h & 1) != 0
-            taps = [jnp.broadcast_to(weights[index, m : m + 1, :], (8, LANES)) for m in range(TAPS)]
-            for part in range(2):
-                plane = part * 4 + tile
-                need = count + 3
-                base = pl.multiple_of((seg * 16 + first) * 8, 8)
-                load = lambda i: focus[plane, pl.ds(base + i * 8, 8), :]
-                tiles = [load(i) for i in range(need + 8)]
-                step = [
-                    jnp.where(eight, tiles[i + 8], tiles[i]) if i < need else tiles[i]
-                    for i in range(need + 7)
-                ]
-                step = [jnp.where(four, step[i + 4], step[i]) for i in range(need + 3)]
-                step = [jnp.where(two, step[i + 2], step[i]) for i in range(need + 1)]
-                for i in range(need):
-                    window[part, i * 8 : i * 8 + 8, :] = jnp.where(one, step[i + 1], step[i])
-                for i in range(count):
-                    total = None
-                    for m in range(TAPS):
-                        term = taps[m] * window[part, i * 8 + 5 + m : i * 8 + 13 + m, :]
-                        total = term if total is None else total + term
-                    out_ref[part, pl.ds(base + i * 8, 8), pl.ds(pl.multiple_of(tile * LANES, LANES), LANES)] = total
-            return carry
-
-        lax.fori_loop(0, 4, body, 0)
+        map_rows(out_ref, focus, weights, coarse, window, seg, first, count)
 
     def halo(towards, source_row, target_row, which):
         def piece(plane, start, count):
@@ -385,10 +389,6 @@
 
     stolt(0, 0, EARLY)
     focus_rows(1)
-    stolt(0, EARLY, 16 - EARLY)
-    stolt(1, 0, EARLY)
-    stolt(1, EARLY, 16 - EARLY)
-    stolt(2, 0, 1)
     to_down.wait_send()
     to_up.wait_send()
     for chunk in range(CHUNKS):
@@ -396,8 +396,33 @@
         all_of(spec_flat, back_flat, send2, recv2, chunk).wait_send()
 
 
+LATE = ((0, EARLY, 16 - EARLY), (1, 0, EARLY), (1, EARLY, 16 - EARLY), (2, 0, 1))
+
+
+def finish(part_ref, focus, weights, coarse, out_hbm, late, window, store_sem):
+    copies = []
+
+    def store(source, first, end):
+        rows = pl.ds(first, end - first)
+        copies.append(
+            pltpu.make_async_copy(
+                source.at[:, rows], out_hbm.at[:, rows], store_sem.at[len(copies)]
+            )
+        )
+        copies[-1].start()
+
+    store(part_ref, 0, EARLY * 8)
+    store(part_ref, (2 * 16 + 1) * 8, ROWS)
+    for seg, first, count in LATE:
+        map_rows(late, focus, weights, coarse, window, seg, first, count)
+        store(late, (seg * 16 + first) * 8, (seg * 16 + first + count) * 8)
+    for copy in copies:
+        copy.wait()
+
+
 def on_device(echo_data, chirp_phase, stolt_shift, tap_index):
     tables = [jnp.asarray(table) for table in dft_tables()]
+    vmem_spec = pl.BlockSpec(memory_space=pltpu.VMEM)
     hbm_spec = pl.BlockSpec(memory_space=pltpu.HBM)
     f32 = jnp.float32
     chirp = chirp_phase.reshape(ROWS // LANES, LANES)
@@ -405,11 +430,16 @@
         pltpu.with_memory_space_constraint(operand, pltpu.HBM)
         for operand in (echo_data, chirp, stolt_shift, tap_index, *tables)
     ]
-    return pl.pallas_call(
+    first = pl.pallas_call(
         kernel,
-        out_shape=pltpu.VMEM((2, ROWS, COLS), f32),
+        out_shape=[
+            pltpu.VMEM((2, ROWS, COLS), f32),
+            pltpu.VMEM((8, FOCUS_ROWS, LANES), f32),
+            pltpu.VMEM((16, 16, LANES), f32),
+            pltpu.VMEM((16, 8, LANES), jnp.int32),
+        ],
         in_specs=[hbm_spec] * 9,
-        out_specs=pl.BlockSpec(memory_space=pltpu.VMEM),
+        out_specs=[vmem_spec] * 4,
         scratch_shapes=[
             pltpu.VMEM((2, ROWS, COLS), f32),
             pltpu.VMEM((ROWS // LANES, LANES), f32),
@@ -426,9 +456,6 @@
             pltpu.VMEM((FLAT, LANES), f32),
             pltpu.VMEM((4, ROWS, LANES), f32),
             pltpu.VMEM((4, ROWS, LANES), f32),
-            pltpu.VMEM((8, FOCUS_ROWS, LANES), f32),
-            pltpu.VMEM((16, 16, LANES), f32),
-            pltpu.VMEM((16, 8, LANES), jnp.int32),
             pltpu.VMEM((ROWS, LANES), f32),
             pltpu.VMEM((ROWS, LANES), f32),
             pltpu.VMEM((2, 160, LANES), f32),
@@ -445,6 +472,18 @@
             collective_id=0, has_side_effects=True, vmem_limit_bytes=50 << 20
         ),
     )(*operands)
+    return pl.pallas_call(
+        finish,
+        out_shape=jax.ShapeDtypeStruct((2, ROWS, COLS), f32),
+        in_specs=[vmem_spec] * 4,
+        out_specs=hbm_spec,
+        scratch_shapes=[
+            pltpu.VMEM((2, ROWS, COLS), f32),
+            pltpu.VMEM((2, 160, LANES), f32),
+            pltpu.SemaphoreType.DMA((2 + len(LATE),)),
+        ],
+        compiler_params=pltpu.CompilerParams(vmem_limit_bytes=16 << 20),
+    )(*first)
 
 
 def solution(mesh):

time: 106 us -> 105 us (level)
  local copies, waits for them, and re-layouts: 1.32 us -> 0 us
    unnamed x1 -> x0, local copies, waits for them, and re-layouts: 1.32 us -> none
    pallas_call x1 -> x2, Pallas kernels: 105 us -> 105 us  [the longest x1 103 us: on_device(): pl.pallas_call(kernel, out_shape=[pltpu.VMEM((2, ROWS, COLS), f32), pltpu...]
where the time goes in v5:
time: 105 us
  Pallas kernels  105 us (100%)
    pallas_call x1, Pallas kernels, on_device(): pl.pallas_call(kernel, out_shape=[pltpu.VMEM((2, ROWS, COLS), f32), pltpu...  103 us

profile of v5, /device:TPU:1, one launch (start us, length us, event | category | flops | bytes accessed | tf_op | source)
XLA Modules:
  0.0 105.4 jit_solution(9665257052469055648)
XLA Ops:
  0.0 103.4 %shard_map.91 = (f32[2,512,512]{2,1,0:T(8,128)S(1)}, f32[8,600,128]{2,1,0:T(8,128)S(1)}, f32[16,16,128]{2,1,0:T(8,128)S(1)}, s32[16,8,128]{2,1,0:T(8,128)S(1)}) custom-call(f32[2,512,512]{2,1,0:T(8,128)} %echo_hbm.1, f32[4,128]{1,0:T(4,128)} %bitcast.1, s32[4,512]{1,0:T(4,128)} %shift_hbm.1, s32[4,512]{1,0:T(4,128)} %tap_hbm.1, ...), custom_call_target="tpu_custom_call" | custom-call | tf_op jit(solution)/shard_map/pallas_call | solution.py:433
  103.4 2.0 %shard_map.92 = f32[2,512,512]{2,1,0:T(8,128)} custom-call(f32[2,512,512]{2,1,0:T(8,128)S(1)} %get-tuple-element.9.part_ref, f32[8,600,128]{2,1,0:T(8,128)S(1)} %get-tuple-element.10.focus, f32[16,16,128]{2,1,0:T(8,128)S(1)} %get-tuple-element.11.weights, s32[16,8,128]{2,1,0:T(8,128)S(1)} %get-tuple-element.12.coarse), custom_call_target="tpu_custom_call" | custom-call | tf_op jit(solution)/shard_map/pallas_call | solution.py:475

commit v6 on v5

--- a/solution.py
+++ b/solution.py
@@ -28,6 +28,8 @@
 FOCUS_ROWS = BEFORE + ROWS + AFTER + 8
 TAPS = 15
 EARLY = 7
+LAST = 1
+HALF_TILES = 8
 
 
 def split(array):
@@ -129,7 +131,7 @@
     out_ref, focus, weights, coarse,
     echo, chirp_ref, shift_ref, tap_ref, t1h, t1l, t2h, t2l, tw, out_flat, in_flat, spec_flat, back_flat, phase_cos, phase_sin,
     chirp_cos, chirp_sin, window,
-    load_sem, table_sem, send1, recv1, send2, recv2, halo_send, halo_recv,
+    load_sem, table_sem, send1, recv1, send2, recv2, halo_send, halo_recv, half_send, half_recv,
 ):
     me = lax.axis_index("az")
     rg = lax.axis_index("rg")
@@ -216,6 +218,41 @@
         lax.fori_loop(1, N_AZ, body, 0)
         home = pl.multiple_of(chunk * CHUNK_FLAT + me * BLOCK, BLOCK)
         target[pl.ds(home, BLOCK), :] = source[pl.ds(home, BLOCK), :]
+
+    def half_row(half, device):
+        return pl.multiple_of(LAST * CHUNK_FLAT + half * CHUNK_FLAT // 2 + device * 8, 8)
+
+    def own_row(half, device):
+        return pl.multiple_of(LAST * CHUNK_FLAT + device * BLOCK + half * 8, 8)
+
+    def exchange_half(source, source_row, target, target_row, send, recv, half, beside=None):
+        def body(i, carry):
+            other = lax.rem(me + i, N_AZ)
+            pltpu.make_async_remote_copy(
+                src_ref=source.at[pl.ds(source_row(half, other), 8)],
+                dst_ref=target.at[pl.ds(target_row(half, me), 8)],
+                send_sem=send,
+                recv_sem=recv,
+                device_id=(other, rg),
+                device_id_type=MESH,
+            ).start()
+            if beside is not None:
+                beside(i - 1)
+            return carry
+
+        lax.fori_loop(1, N_AZ, body, 0)
+        target[pl.ds(target_row(half, me), 8), :] = source[pl.ds(source_row(half, me), 8), :]
+
+    def half_of(half):
+        rows = pl.ds(LAST * CHUNK_FLAT + half * CHUNK_FLAT // 2, CHUNK_FLAT // 2 - 8)
+        return pltpu.make_async_remote_copy(
+            src_ref=spec_flat.at[rows],
+            dst_ref=back_flat.at[rows],
+            send_sem=half_send.at[half],
+            recv_sem=half_recv.at[half],
+            device_id=(lax.rem(me + 1, N_AZ), rg),
+            device_id_type=MESH,
+        )
 
     def all_of(source, target, send, recv, chunk):
         rows = pl.ds(pl.multiple_of(chunk * CHUNK_FLAT, BLOCK), CHUNK_FLAT - BLOCK)
@@ -301,13 +338,30 @@
                     spec_flat[pl.ds(start + pair * 8 + quarter * 2 + half, N_AZ, stride=BLOCK), :] = (
                         final[quarter * N_AZ : (quarter + 1) * N_AZ, half * LANES : (half + 1) * LANES]
                     )
-        exchange(spec_flat, back_flat, send2, recv2, chunk)
+
+        @pl.when(chunk != LAST)
+        def _():
+            exchange(spec_flat, back_flat, send2, recv2, chunk)
+
+        @pl.when(chunk == LAST)
+        def _():
+            for half in (1, 0):
+                exchange_half(
+                    spec_flat, own_row, back_flat, half_row,
+                    half_send.at[half], half_recv.at[half], half,
+                )
 
     def focus_rows(chunk):
         all_of(spec_flat, back_flat, send2, recv2, chunk).wait_recv()
-
+        focus_tiles(chunk * 16, 16)
+
+    def focus_half(half):
+        half_of(half).wait_recv()
+        focus_tiles(LAST * 16 + half * HALF_TILES, HALF_TILES)
+
+    def focus_tiles(first, count):
         def body(i, carry):
-            row = pl.multiple_of(chunk * CHUNK_ROWS + i * 8, 8)
+            row = pl.multiple_of((first + i) * 8, 8)
             for tile in range(4):
                 a = back_flat[pl.ds(row * 8 + tile, 8, stride=8), :]
                 b = back_flat[pl.ds(row * 8 + 4 + tile, 8, stride=8), :]
@@ -317,7 +371,7 @@
                 focus[4 + tile, pl.ds(BEFORE + row, 8), :] = a * s + b * c
             return carry
 
-        lax.fori_loop(0, CHUNK_ROWS // 8, body, 0)
+        lax.fori_loop(0, count, body, 0)
 
     def stolt(seg, first, count):
         map_rows(out_ref, focus, weights, coarse, window, seg, first, count)
@@ -357,7 +411,9 @@
 
         @pl.when(k == 1)
         def _():
-            exchange(out_flat, in_flat, send1, recv1, 1, beside=send_down)
+            first = out_flat, half_row, in_flat, own_row, send1.at[LAST], recv1.at[LAST]
+            exchange_half(*first, 0, beside=send_down)
+            exchange_half(*first, 1)
             for piece in range(N_AZ - 1, 72):
                 send_down(piece)
 
@@ -388,15 +444,21 @@
         focus[:, pl.ds(0, BEFORE), :] = jnp.zeros((8, BEFORE, LANES), jnp.float32)
 
     stolt(0, 0, EARLY)
-    focus_rows(1)
+    focus_half(1)
+    stolt(LAST, HALF_TILES + 1, 7)
+    stolt(2, 0, 1)
+    focus_half(0)
     to_down.wait_send()
     to_up.wait_send()
     for chunk in range(CHUNKS):
         all_of(out_flat, in_flat, send1, recv1, chunk).wait_send()
-        all_of(spec_flat, back_flat, send2, recv2, chunk).wait_send()
-
-
-LATE = ((0, EARLY, 16 - EARLY), (1, 0, EARLY), (1, EARLY, 16 - EARLY), (2, 0, 1))
+        if chunk != LAST:
+            all_of(spec_flat, back_flat, send2, recv2, chunk).wait_send()
+    for half in range(2):
+        half_of(half).wait_send()
+
+
+LATE = ((0, EARLY, 16 - EARLY), (LAST, 0, HALF_TILES + 1))
 
 
 def finish(part_ref, focus, weights, coarse, out_hbm, late, window, store_sem):
@@ -412,7 +474,7 @@
         copies[-1].start()
 
     store(part_ref, 0, EARLY * 8)
-    store(part_ref, (2 * 16 + 1) * 8, ROWS)
+    store(part_ref, (LAST * 16 + HALF_TILES + 1) * 8, ROWS)
     for seg, first, count in LATE:
         map_rows(late, focus, weights, coarse, window, seg, first, count)
         store(late, (seg * 16 + first) * 8, (seg * 16 + first + count) * 8)
@@ -467,6 +529,8 @@
             pltpu.SemaphoreType.DMA((CHUNKS,)),
             pltpu.SemaphoreType.DMA((2,)),
             pltpu.SemaphoreType.DMA((2,)),
+            pltpu.SemaphoreType.DMA((2,)),
+            pltpu.SemaphoreType.DMA((2,)),
         ],
         compiler_params=pltpu.CompilerParams(
             collective_id=0, has_side_effects=True, vmem_limit_bytes=50 << 20

time: 105 us -> 105 us (level)
  no operation moved by 1% of the time
where the time goes in v6:
time: 105 us
  Pallas kernels  105 us (100%)
    pallas_call x1, Pallas kernels, on_device(): pl.pallas_call(kernel, out_shape=[pltpu.VMEM((2, ROWS, COLS), f32), pltpu...  104 us

profile of v6, /device:TPU:1, one launch (start us, length us, event | category | flops | bytes accessed | tf_op | source)
XLA Modules:
  0.0 105.3 jit_solution(14872464677504274362)
XLA Ops:
  0.0 103.7 %shard_map.91 = (f32[2,512,512]{2,1,0:T(8,128)S(1)}, f32[8,600,128]{2,1,0:T(8,128)S(1)}, f32[16,16,128]{2,1,0:T(8,128)S(1)}, s32[16,8,128]{2,1,0:T(8,128)S(1)}) custom-call(f32[2,512,512]{2,1,0:T(8,128)} %echo_hbm.1, f32[4,128]{1,0:T(4,128)} %bitcast.1, s32[4,512]{1,0:T(4,128)} %shift_hbm.1, s32[4,512]{1,0:T(4,128)} %tap_hbm.1, ...), custom_call_target="tpu_custom_call" | custom-call | tf_op jit(solution)/shard_map/pallas_call | solution.py:495
  103.7 1.6 %shard_map.92 = f32[2,512,512]{2,1,0:T(8,128)} custom-call(f32[2,512,512]{2,1,0:T(8,128)S(1)} %get-tuple-element.9.part_ref, f32[8,600,128]{2,1,0:T(8,128)S(1)} %get-tuple-element.10.focus, f32[16,16,128]{2,1,0:T(8,128)S(1)} %get-tuple-element.11.weights, s32[16,8,128]{2,1,0:T(8,128)S(1)} %get-tuple-element.12.coarse), custom_call_target="tpu_custom_call" | custom-call | tf_op jit(solution)/shard_map/pallas_call | solution.py:539

commit v7 on v6

--- a/solution.py
+++ b/solution.py
@@ -140,6 +140,17 @@
 
     barrier = pltpu.get_barrier_semaphore()
 
+    def moved(dz, rest):
+        x, z, core = me // 16, me // 2 % 8, me % 2
+        return ((x + rest // 2) % 4 * 8 + (z + dz) % 8) * 2 + (core + rest) % 2
+
+    def around(i):
+        return lax.rem(me + i, N_AZ)
+
+    def nearest_first(i):
+        rank = 7 - i // 8
+        return moved(4 + (1 - rank % 2 * 2) * ((rank + 1) // 2), i % 8)
+
     def greet(i, carry):
         pl.semaphore_signal(
             barrier, inc=1, device_id=(lax.rem(me + i, N_AZ), rg), device_id_type=MESH
@@ -198,9 +209,9 @@
 
         lax.fori_loop(0, CHUNK_ROWS // 8, body, 0)
 
-    def exchange(source, target, send, recv, chunk, beside=None):
+    def exchange(source, target, send, recv, chunk, others=around):
         def body(i, carry):
-            other = lax.rem(me + i, N_AZ)
+            other = others(i)
             away = pl.multiple_of(chunk * CHUNK_FLAT + other * BLOCK, BLOCK)
             home = pl.multiple_of(chunk * CHUNK_FLAT + me * BLOCK, BLOCK)
             pltpu.make_async_remote_copy(
@@ -211,8 +222,6 @@
                 device_id=(other, rg),
                 device_id_type=MESH,
             ).start()
-            if beside is not None:
-                beside(i - 1)
             return carry
 
         lax.fori_loop(1, N_AZ, body, 0)
@@ -225,9 +234,11 @@
     def own_row(half, device):
         return pl.multiple_of(LAST * CHUNK_FLAT + device * BLOCK + half * 8, 8)
 
-    def exchange_half(source, source_row, target, target_row, send, recv, half, beside=None):
+    def exchange_half(
+        source, source_row, target, target_row, send, recv, half, others=around, beside=None
+    ):
         def body(i, carry):
-            other = lax.rem(me + i, N_AZ)
+            other = others(i)
             pltpu.make_async_remote_copy(
                 src_ref=source.at[pl.ds(source_row(half, other), 8)],
                 dst_ref=target.at[pl.ds(target_row(half, me), 8)],
@@ -268,7 +279,7 @@
     echo_copies[0].wait()
     matched(0)
     pl.semaphore_wait(barrier, N_AZ + 1)
-    exchange(out_flat, in_flat, send1, recv1, 0)
+    exchange(out_flat, in_flat, send1, recv1, 0, nearest_first)
     echo_copies[3].wait()
     matched(3)
     exchange(out_flat, in_flat, send1, recv1, 3)

time: 105 us -> 106 us (level)
  no operation moved by 1% of the time
where the time goes in v7:
time: 106 us; the launch traced here: 105 us
  Pallas kernels  105 us (99%)
    pallas_call x1, Pallas kernels, on_device(): pl.pallas_call(kernel, out_shape=[pltpu.VMEM((2, ROWS, COLS), f32), pltpu...  104 us

profile of v7, /device:TPU:1, one launch (start us, length us, event | category | flops | bytes accessed | tf_op | source)
XLA Modules:
  0.0 105.4 jit_solution(15979125407876195425)
XLA Ops:
  0.0 103.8 %shard_map.91 = (f32[2,512,512]{2,1,0:T(8,128)S(1)}, f32[8,600,128]{2,1,0:T(8,128)S(1)}, f32[16,16,128]{2,1,0:T(8,128)S(1)}, s32[16,8,128]{2,1,0:T(8,128)S(1)}) custom-call(f32[2,512,512]{2,1,0:T(8,128)} %echo_hbm.1, f32[4,128]{1,0:T(4,128)} %bitcast.1, s32[4,512]{1,0:T(4,128)} %shift_hbm.1, s32[4,512]{1,0:T(4,128)} %tap_hbm.1, ...), custom_call_target="tpu_custom_call" | custom-call | tf_op jit(solution)/shard_map/pallas_call | solution.py:506
  103.8 1.6 %shard_map.92 = f32[2,512,512]{2,1,0:T(8,128)} custom-call(f32[2,512,512]{2,1,0:T(8,128)S(1)} %get-tuple-element.9.part_ref, f32[8,600,128]{2,1,0:T(8,128)S(1)} %get-tuple-element.10.focus, f32[16,16,128]{2,1,0:T(8,128)S(1)} %get-tuple-element.11.weights, s32[16,8,128]{2,1,0:T(8,128)S(1)} %get-tuple-element.12.coarse), custom_call_target="tpu_custom_call" | custom-call | tf_op jit(solution)/shard_map/pallas_call | solution.py:550
